TPU v7x, 32 devices: a whole 2x2x4 slice. The times are simulated.
32 devices in a mesh: rep: 2 (over x), row: 4 (over z), col: 4 (over y, core).
Axes of the slice: x: 2, y: 2, z: 4, core: 2. Of those that a mesh axis runs over, the one named last changes fastest.
Arguments:
- coordinates: bfloat16 [8, 32, 3, 128], P('rep')
- resample: int32 [2, 22], P('rep'), may hold values from 0 to 7, as said below
- block_slot: int32 [8], replicated, may hold values from 0 to 7, as said below
- lag_time: int32 [2], P('rep'), may hold values from 1 to 8
- atom_pairs: int32 [2, 4096], replicated, may hold values from 0 to 127, as said below
Outputs:
- instant_cov: bfloat16 [2, 4096, 4096], P('rep', 'row', 'col')
- lagged_cov: bfloat16 [2, 4096, 4096], P('rep', 'row', 'col')
Inputs may be any that keep to these rules, and one draw needn't show every extreme that they name: `resample`: the owner of a block is block_slot // 4. In each replicate at most 16 draws have one owner, and some owner has exactly 16; a block may be drawn more than once. `block_slot`: each slot holds exactly one block. `atom_pairs`: the two atoms of a feature differ, and no unordered pair of atoms appears twice.
All inputs are finite; a program needn't handle non-finite values.
Results may differ from a plain program's by a relative error of at most 0.0073.
Values may be sent and summed in bfloat16 or wider, within the bound.
A program may use at most 64 MiB of HBM per device.

v0:
```python
import jax
import jax.numpy as jnp
from jax import lax
from jax.sharding import PartitionSpec as P

F = 4096
ATOMS = 128
BLOCK_LEN = 32
DRAWS = 22


def slot_lookup(lists, slot_table):
    matches = lists[..., None] == jnp.arange(slot_table.shape[0], dtype=jnp.int32)
    return jnp.sum(jnp.where(matches, slot_table, 0), axis=-1)


def owner_rank(lists, slot_table, blk_count):
    slots = slot_lookup(lists, slot_table)
    owner_ids = slots // blk_count
    local_ids = slots % blk_count
    draw_ids = jnp.arange(lists.shape[-1], dtype=jnp.int32)
    before = (owner_ids[..., :, None] == owner_ids[..., None, :]) & (
        draw_ids[None, :] < draw_ids[:, None]
    )
    ranks = jnp.sum(before.astype(jnp.int32), axis=-1)
    return (owner_ids, local_ids, ranks)


def pack_requests(resample, block_slot, local_data, capacity):
    every_list = lax.all_gather(resample, "rep", axis=0, tiled=True)
    blk_count = local_data.shape[0]
    owners_all, local_all, ranks_all = owner_rank(every_list, block_slot, blk_count)
    myself = lax.axis_index("rep")
    wanted = (owners_all == myself)[:, :, None] & (
        ranks_all[:, :, None] == jnp.arange(capacity, dtype=jnp.int32)
    )
    picked = local_all[:, :, None] == jnp.arange(blk_count, dtype=jnp.int32)
    selector = jnp.einsum(
        "rdc,rdk->rck", wanted.astype(jnp.float32), picked.astype(jnp.float32)
    ).astype(jnp.bfloat16)
    return jnp.einsum(
        "rck,kx->rcx", selector, local_data, preferred_element_type=jnp.float32
    ).astype(jnp.bfloat16)


def unpack_blocks(received, resample, block_slot, blk_count, capacity):
    owner_ids, local_ids, ranks = owner_rank(resample[0], block_slot, blk_count)
    rows_wanted = owner_ids * capacity + ranks
    flat = received.reshape(-1, received.shape[-1])
    return jnp.take(flat, rows_wanted, axis=0)


def tile_features(chosen, atom_pairs, first_feature, width, shift):
    first_atoms = lax.dynamic_slice_in_dim(atom_pairs[0], first_feature, width)
    second_atoms = lax.dynamic_slice_in_dim(atom_pairs[1], first_feature, width)
    atom_ids = jnp.arange(chosen.shape[-1], dtype=jnp.int32)[:, None]
    signed = (
        (atom_ids == first_atoms[None, :]).astype(jnp.float32)
        - (atom_ids == second_atoms[None, :]).astype(jnp.float32)
    ).astype(jnp.bfloat16)
    flat = chosen.reshape(-1, chosen.shape[-1])
    difference = jnp.dot(flat, signed, preferred_element_type=jnp.float32).reshape(
        DRAWS, BLOCK_LEN, 3, width
    )
    squared = (
        difference[:, :, 0] * difference[:, :, 0]
        + difference[:, :, 1] * difference[:, :, 1]
        + difference[:, :, 2] * difference[:, :, 2]
    )
    features = jnp.sqrt(squared).astype(jnp.bfloat16)
    doubled = jnp.concatenate([features, features], axis=1)
    shifted = lax.dynamic_slice_in_dim(doubled, shift, BLOCK_LEN, axis=1)
    valid_rows = (jnp.arange(BLOCK_LEN, dtype=jnp.int32) < BLOCK_LEN - shift)[None, :, None]
    pair_count = (2 * DRAWS * (BLOCK_LEN - shift)).astype(jnp.float32)
    earlier = jnp.where(valid_rows, features.astype(jnp.float32), 0.0)
    later = jnp.where(valid_rows, shifted.astype(jnp.float32), 0.0)
    feature_mean = (jnp.sum(earlier, axis=(0, 1)) + jnp.sum(later, axis=(0, 1))) / pair_count
    zero_lag = (
        jnp.where(valid_rows, earlier - feature_mean, 0.0).astype(jnp.bfloat16).reshape(-1, width)
    )
    lagged = (
        jnp.where(valid_rows, later - feature_mean, 0.0).astype(jnp.bfloat16).reshape(-1, width)
    )
    return (zero_lag, lagged, pair_count)


def shards(coordinates, resample, block_slot, lag_time, atom_pairs):
    rep_total = lax.axis_size("rep")
    per_owner = (DRAWS + rep_total - 1) // rep_total
    capacity = max(2, per_owner + per_owner // 2)
    blk_count = coordinates.shape[0]
    outgoing = pack_requests(resample, block_slot, coordinates.reshape(blk_count, -1), capacity)
    received = lax.all_to_all(outgoing, "rep", split_axis=0, concat_axis=0, tiled=True)
    chosen = unpack_blocks(received, resample, block_slot, blk_count, capacity).reshape(
        DRAWS, BLOCK_LEN, 3, ATOMS
    )
    width = F // lax.axis_size("row")
    shift = lag_time[0]
    zero_row, lag_row, pair_count = tile_features(
        chosen, atom_pairs, lax.axis_index("row") * width, width, shift
    )
    row_stack = jnp.concatenate([zero_row, lag_row], axis=0)
    zero_col, lag_col, unused_count = tile_features(
        chosen, atom_pairs, lax.axis_index("col") * width, width, shift
    )
    col_stack = jnp.concatenate([zero_col, lag_col], axis=0)
    half_rows = col_stack.shape[0] // 2
    mirrored = jnp.concatenate([col_stack[half_rows:], col_stack[:half_rows]], axis=0)
    instant = (
        jnp.einsum("na,nb->ab", row_stack, col_stack, preferred_element_type=jnp.float32)
        / pair_count
    )
    crossed = (
        jnp.einsum("na,nb->ab", row_stack, mirrored, preferred_element_type=jnp.float32)
        / pair_count
    )
    return (instant[None].astype(jnp.bfloat16), crossed[None].astype(jnp.bfloat16))


def solution(mesh):
    return jax.shard_map(
        shards,
        mesh=mesh,
        in_specs=(P("rep", None, None, None), P("rep", None), P(), P("rep"), P()),
        out_specs=(P("rep", "row", "col"), P("rep", "row", "col")),
        check_vma=False,
    )
```

profile of v0, /device:TPU:0, one launch (start us, length us, event | category | flops | bytes accessed | tf_op | source)
XLA Modules:
  0.0 51.9 jit_solution(10854731796667606534)
XLA Ops:
  0.6 0.0 copy-start.2
  0.6 0.0 copy-start.1
  0.7 0.0 copy-start
  0.7 5.3 %all-gather = s32[2,1,22]{2,1,0:T(1,128)S(1)} all-gather(s32[1,1,22]{2,1,0:T(1,128)} %bitcast.66), channel_id=1, replica_groups=mesh['rep'=2,'row'=4,'col'=4] {'rep'}, dimensions={0}, use_global_device_ids=true | all-gather | bytes 264 | tf_op jit(solution)/shard_map/all_gather | solution.py:30
  6.0 0.7 %select_reduce_fusion.2 = s32[2,22]{1,0:T(2,128)S(1)} fusion(s32[8]{0:T(128)} %param.7, s32[2,22]{1,0:T(2,128)S(1)} %bitcast.65), kind=kLoop, calls=%fused_computation.76 | loop fusion | flops 1012 | bytes 384 | tf_op jit(solution)/shard_map/reduce_sum | solution.py:14
  6.8 0.1 copy.23
  6.9 0.5 fusion.44
  7.4 0.1 copy.24
  7.5 1.0 %copy.25 = bf16[4,32,3,128]{3,2,1,0:T(4,128)(2,1)S(1)} copy(bf16[4,32,3,128]{3,1,2,0:T(8,128)(2,1)} %param.5) | data formatting | bytes 196608 | tf_op args[0]
  8.4 0.1 reshape.274
  8.5 1.5 %convolution_convert_fusion = bf16[2,16,12288]{2,1,0:T(8,128)(2,1)} fusion(bf16[4,12288,1]{1,0,2:T(4,128)(2,1)S(1)} %reshape.274, s32[2,22]{1,0:T(2,128)S(1)} %copy.24, pred[2,22]{1,0:T(4,128)(4,1)S(1)} %get-tuple-element.6, s32[2,22]{1,0:T(2,128)S(1)} %and_select_fusion.1), kind=kOutput, calls=%fused_computation.1 | convolution fusion | flops 3546288 | bytes 885132 | tf_op jit(solution)/shard_map/rck,kx->rcx/dot_general | solution.py:41
  10.0 3.5 %all-to-all-start = ((bf16[2,16,12288]{2,1,0:T(8,128)(2,1)}), bf16[2,16,12288]{2,1,0:T(8,128)(2,1)S(1)}, u32[]{:S(2)}, u32[]{:S(2)}) async-start(bf16[2,16,12288]{2,1,0:T(8,128)(2,1)} %convolution_convert_fusion), calls=%async_computation | async-start | bytes 1572864 | tf_op jit(solution)/shard_map/all_to_all | solution.py:93
  13.5 0.0 copy-done
  13.6 0.0 copy-done.2
  13.6 0.1 select_reduce_fusion.3
  13.7 0.2 convert_reduce_fusion
  14.6 0.1 broadcast_in_dim.106
  14.7 9.0 %all-to-all-done = bf16[2,16,12288]{2,1,0:T(8,128)(2,1)S(1)} async-done(((bf16[2,16,12288]{2,1,0:T(8,128)(2,1)}), bf16[2,16,12288]{2,1,0:T(8,128)(2,1)S(1)}, u32[]{:S(2)}, u32[]{:S(2)}) %all-to-all-start) | async-done | bytes 786464 | tf_op jit(solution)/shard_map/all_to_all | solution.py:93
  23.7 0.9 %gather_fusion = bf16[22,12288]{1,0:T(8,128)(2,1)S(1)} fusion(bf16[32,12288]{1,0:T(8,128)(2,1)S(1)} %bitcast.56, s32[1024]{0:T(1024)S(1)} %pad_clamp_fusion), kind=kCustom, calls=%fused_computation | custom fusion | bytes 1081432 | tf_op jit(solution)/shard_map/jit(_take)/gather | solution.py:50
  24.6 0.8 %gather.7 = bf16[22,32,3,128]{3,2,1,0:T(4,128)(2,1)S(1)} reshape(bf16[22,12288]{1,0:T(8,128)(2,1)S(1)} %gather_fusion) | data formatting | bytes 1081344 | tf_op jit(solution)/shard_map/jit(_take)/gather | solution.py:50
  25.4 0.4 broadcast_select_fusion
  25.8 1.3 %fusion.32 = f32[22,32,3,1024]{3,1,0,2:T(8,128)S(1)} fusion(bf16[22,32,3,128]{3,2,1,0:T(4,128)(2,1)S(1)} %broadcast_select_fusion, s32[1024]{0:T(1024)S(1)} %bitcast.64, s32[1024]{0:T(1024)S(1)} %bitcast.62), kind=kOutput, calls=%fused_computation.53 | convolution fusion | flops 554434560 | bytes 9199616 | tf_op jit(solution)/shard_map/dot_general | solution.py:62
  27.1 1.2 %fusion.59 = bf16[22,32,1024]{2,1,0:T(8,128)(2,1)S(1)} fusion(f32[22,32,3,1024]{3,1,0,2:T(8,128)S(1)} %fusion.32), kind=kLoop, calls=%fused_computation.116 | loop fusion | flops 4325376 | bytes 10092544 | tf_op jit(solution)/shard_map/sqrt | solution.py:70
  28.3 1.2 %fusion.2 = bf16[22,32,1,1024]{3,1,0,2:T(8,128)(2,1)S(1)} fusion(f32[22,32,3,1024]{3,1,0,2:T(8,128)S(1)} %fusion.32), kind=kLoop, calls=%fused_computation.7 | loop fusion | flops 4325376 | bytes 10092544 | tf_op jit(solution)/shard_map/convert.1
  29.5 1.3 %fusion.34 = f32[22,32,3,1024]{3,1,2,0:T(8,128)S(1)} fusion(bf16[22,32,3,128]{3,2,1,0:T(4,128)(2,1)S(1)} %broadcast_select_fusion, s32[1024]{0:T(1024)S(1)} %bitcast.63, s32[1024]{0:T(1024)S(1)} %bitcast.61), kind=kOutput, calls=%fused_computation.55 | convolution fusion | flops 554434560 | bytes 9199616 | tf_op jit(solution)/shard_map/dot_general | solution.py:62
  30.9 1.2 %fusion.60 = bf16[22,32,1024]{2,1,0:T(8,128)(2,1)S(1)} fusion(f32[22,32,3,1024]{3,1,2,0:T(8,128)S(1)} %fusion.34), kind=kLoop, calls=%fused_computation.117 | loop fusion | flops 4325376 | bytes 10092544 | tf_op jit(solution)/shard_map/sqrt | solution.py:70
  32.1 1.2 %fusion.6 = bf16[22,32,1,1024]{3,1,2,0:T(8,128)(2,1)S(1)} fusion(f32[22,32,3,1024]{3,1,2,0:T(8,128)S(1)} %fusion.34), kind=kLoop, calls=%fused_computation.14 | loop fusion | flops 4325376 | bytes 10092544 | tf_op jit(solution)/shard_map/convert.3
  33.3 5.2 %fusion.23 = (f32[1024]{0:T(1024)S(1)}, f32[1024]{0:T(1024)S(1)}, f32[1024]{0:T(1024)S(1)}, f32[1024]{0:T(1024)S(1)}) fusion(pred[32]{0:T(512)(128)(4,1)S(1)} %iota_compare_fusion.11, s32[]{:T(128)S(6)} %select_n.137, bf16[22,32,1024]{2,1,0:T(8,128)(2,1)S(1)} %fusion.60, bf16[22,32,1024]{2,1,0:T(8,128)(2,1)S(1)} %fusion.59, ...), kind=kLoop, calls=%fused_computation.45 | loop fusion | flops 21622784 | bytes 20201508 | tf_op jit(solution)/shard_map/reduce_sum | solution.py:77
  38.5 2.6 %select_convert_fusion.1 = (bf16[22,32,1024]{2,1,0:T(8,128)(2,1)S(1)}, bf16[22,32,1024]{2,1,0:T(8,128)(2,1)S(1)}) fusion(f32[1024]{0:T(1024)S(1)} %get-tuple-element.19, pred[32]{0:T(512)(128)(4,1)S(1)} %iota_compare_fusion.11, s32[]{:T(128)S(6)} %select_n.137, bf16[22,32,1024]{2,1,0:T(8,128)(2,1)S(1)} %fusion.60, f32[1024]{0:T(1024)S(1)} %get-tuple-element.18, ...), kind=kLoop, calls=%fused_computation.43 | loop fusion | flops 11534336 | bytes 5775396 | tf_op jit(solution)/shard_map/convert_element_type | solution.py:82
  41.2 1.4 %fusion.21 = (bf16[704,1024]{1,0:T(8,128)(2,1)S(1)}, bf16[704,1024]{1,0:T(8,128)(2,1)S(1)}) fusion(bf16[22,32,1,1024]{3,1,2,0:T(8,128)(2,1)S(1)} %fusion.6, f32[1024]{0:T(1024)S(1)} %get-tuple-element.19, pred[704]{0:T(1024)(128)(4,1)S(1)} %broadcast_in_dim.106, f32[1024]{0:T(1024)S(1)} %get-tuple-element.18, bf16[22,32,1,1024]{3,1,0,2:T(8,128)(2,1)S(1)} %fusion.2), kind=kLoop, calls=%fused_computation.38 | loop fusion | flops 7208960 | bytes 5776064 | tf_op jit(solution)/shard_map/convert_element_type | solution.py:79
  42.6 4.7 %fusion.25 = bf16[1,1024,1024]{2,1,0:T(8,128)(2,1)} fusion(f32[]{:T(128)S(6)} %convert_element_type.94, bf16[704,1024]{1,0:T(8,128)(2,1)S(1)} %get-tuple-element.15, bf16[704,1024]{1,0:T(8,128)(2,1)S(1)} %bitcast.59, bf16[704,1024]{1,0:T(8,128)(2,1)S(1)} %bitcast.57, bf16[704,1024]{1,0:T(8,128)(2,1)S(1)} %get-tuple-element.14), kind=kOutput, calls=%fused_computation.48 | convolution fusion | flops 2966421504 | bytes 7864324 | tf_op jit(solution)/shard_map/na,nb->ab/dot_general | solution.py:114
  47.2 4.6 %fusion.24 = bf16[1,1024,1024]{2,1,0:T(8,128)(2,1)} fusion(f32[]{:T(128)S(6)} %convert_element_type.94, bf16[704,1024]{1,0:T(8,128)(2,1)S(1)} %bitcast.60, bf16[704,1024]{1,0:T(8,128)(2,1)S(1)} %get-tuple-element.15, bf16[704,1024]{1,0:T(8,128)(2,1)S(1)} %bitcast.58, bf16[704,1024]{1,0:T(8,128)(2,1)S(1)} %get-tuple-element.14), kind=kOutput, calls=%fused_computation.47 | convolution fusion | flops 2966421504 | bytes 7864324 | tf_op jit(solution)/shard_map/na,nb->ab/dot_general | solution.py:110
  (14 shorter events, 0.1 us)
Async XLA Ops:
  0.6 12.9 %copy-start.2 = (s32[1,22]{1,0:T(1,128)S(1)}, s32[1,22]{1,0:T(1,128)}, u32[]{:S(2)}) copy-start(s32[1,22]{1,0:T(1,128)} %param.6) | copy-start | bytes 268
  0.6 12.9 %copy-start.1 = (s32[8]{0:T(128)S(1)}, s32[8]{0:T(128)}, u32[]{:S(2)}) copy-start(s32[8]{0:T(128)} %param.7) | copy-start | bytes 100
  0.7 12.9 %copy-start = (s32[2,4096]{1,0:T(2,128)S(1)}, s32[2,4096]{1,0:T(2,128)}, u32[]{:S(2)}) copy-start(s32[2,4096]{1,0:T(2,128)} %param.9) | copy-start | bytes 98308
  10.0 13.7 %all-to-all-start = ((bf16[2,16,12288]{2,1,0:T(8,128)(2,1)}), bf16[2,16,12288]{2,1,0:T(8,128)(2,1)S(1)}, u32[]{:S(2)}, u32[]{:S(2)}) async-start(bf16[2,16,12288]{2,1,0:T(8,128)(2,1)} %convolution_convert_fusion), calls=%async_computation | async-start | bytes 1572864 | tf_op jit(solution)/shard_map/all_to_all | solution.py:93
where the time goes:
time: 52.2 us; the launch traced here: 51.9 us
  other arithmetic  16.1 us (31%)
  matrix products  13.4 us (26%)
  waiting for transfers between devices  8.98 us (17%)
  blocking collectives  5.31 us (10%)
  starting transfers between devices  3.54 us (7%)
  local copies, waits for them, and re-layouts  3.07 us (6%)
  between operations  1.51 us (3%)
    all_to_all x1, waiting for transfers between devices, shards(): lax.all_to_all(outgoing, 'rep', split_axis=0, concat_axis=0, tiled=True)  8.98 us
    all_gather x1, blocking collectives, pack_requests(): every_list = lax.all_gather(resample, 'rep', axis=0, tiled=True)  5.31 us
    reduce_sum x1, other arithmetic, tile_features(): jnp.sum(later, axis=(0, 1))  5.25 us
    dot_general x1, matrix products, shards(): jnp.einsum('na,nb->ab', row_stack, mirrored, preferred_element_type=jnp.f...  4.66 us
    dot_general x1, matrix products, shards(): jnp.einsum('na,nb->ab', row_stack, col_stack, preferred_element_type=jnp....  4.65 us
    all_to_all x1, starting transfers between devices, shards(): lax.all_to_all(outgoing, 'rep', split_axis=0, concat_axis=0, tiled=True)  3.54 us
    convert_element_type x1, other arithmetic, tile_features(): jnp.where(valid_rows, later - feature_mean, 0.0).astype(jnp.bfloat16)  2.63 us
    dot_general x2, matrix products, tile_features(): jnp.dot(flat, signed, preferred_element_type=jnp.float32)  2.62 us
  transfers between devices with their start and end apart: 1, of which 1 were waited for; matrix products, arithmetic and copies ran while one was open for 1% of the time, Pallas kernels for 0%

commit v1 on v0

v1 whole, which is shorter than its diff:
```python
import functools

import jax
import jax.numpy as jnp
from jax import lax
from jax.experimental import pallas as pl
from jax.experimental.pallas import tpu as pltpu
from jax.sharding import PartitionSpec as P

F = 4096
ATOMS = 128
BLOCK_LEN = 32
DRAWS = 22
TILE = 256
MESH = pl.DeviceIdType.MESH


def slot_lookup(lists, slot_table):
    matches = lists[..., None] == jnp.arange(slot_table.shape[0], dtype=jnp.int32)
    return jnp.sum(jnp.where(matches, slot_table, 0), axis=-1)


def owner_rank(lists, slot_table, blk_count):
    slots = slot_lookup(lists, slot_table)
    owner_ids = slots // blk_count
    local_ids = slots % blk_count
    draw_ids = jnp.arange(lists.shape[-1], dtype=jnp.int32)
    before = (owner_ids[..., :, None] == owner_ids[..., None, :]) & (
        draw_ids[None, :] < draw_ids[:, None]
    )
    ranks = jnp.sum(before.astype(jnp.int32), axis=-1)
    return (owner_ids, local_ids, ranks)


def pack_requests(resample, block_slot, local_data, capacity):
    every_list = lax.all_gather(resample, "rep", axis=0, tiled=True)
    blk_count = local_data.shape[0]
    owners_all, local_all, ranks_all = owner_rank(every_list, block_slot, blk_count)
    myself = lax.axis_index("rep")
    wanted = (owners_all == myself)[:, :, None] & (
        ranks_all[:, :, None] == jnp.arange(capacity, dtype=jnp.int32)
    )
    picked = local_all[:, :, None] == jnp.arange(blk_count, dtype=jnp.int32)
    selector = jnp.einsum(
        "rdc,rdk->rck", wanted.astype(jnp.float32), picked.astype(jnp.float32)
    ).astype(jnp.bfloat16)
    return jnp.einsum(
        "rck,kx->rcx", selector, local_data, preferred_element_type=jnp.float32
    ).astype(jnp.bfloat16)


def unpack_blocks(received, resample, block_slot, blk_count, capacity):
    owner_ids, local_ids, ranks = owner_rank(resample[0], block_slot, blk_count)
    rows_wanted = owner_ids * capacity + ranks
    flat = received.reshape(-1, received.shape[-1])
    return jnp.take(flat, rows_wanted, axis=0)


def drawn_blocks(coordinates, resample, block_slot):
    rep_total = lax.axis_size("rep")
    per_owner = (DRAWS + rep_total - 1) // rep_total
    capacity = max(2, per_owner + per_owner // 2)
    blk_count = coordinates.shape[0]
    outgoing = pack_requests(resample, block_slot, coordinates.reshape(blk_count, -1), capacity)
    received = lax.all_to_all(outgoing, "rep", split_axis=0, concat_axis=0, tiled=True)
    return unpack_blocks(received, resample, block_slot, blk_count, capacity).reshape(
        DRAWS, BLOCK_LEN, 3, ATOMS
    )


def swap_kernel(own_ref, other_ref, send_sem, recv_sem):
    partner = {"rep": 1 - lax.axis_index("rep")}
    barrier = pltpu.get_barrier_semaphore()
    pl.semaphore_signal(barrier, inc=1, device_id=partner, device_id_type=MESH)
    pl.semaphore_wait(barrier, 1)
    copy = pltpu.make_async_remote_copy(
        src_ref=own_ref,
        dst_ref=other_ref,
        send_sem=send_sem,
        recv_sem=recv_sem,
        device_id=partner,
        device_id_type=MESH,
    )
    copy.start()
    copy.wait()


def swap(own):
    return pl.pallas_call(
        swap_kernel,
        out_shape=jax.ShapeDtypeStruct(own.shape, own.dtype),
        in_specs=[pl.BlockSpec(memory_space=pl.ANY)],
        out_specs=pl.BlockSpec(memory_space=pl.ANY),
        scratch_shapes=[pltpu.SemaphoreType.DMA, pltpu.SemaphoreType.DMA],
        compiler_params=pltpu.CompilerParams(collective_id=0, has_side_effects=True),
        name="swap",
    )(own)


def dot(a, b, contract=((1,), (0,))):
    return lax.dot_general(a, b, (contract, ((), ())), preferred_element_type=jnp.float32)


def signed_atoms(pairs_ref, first, width):
    ids = lax.broadcasted_iota(jnp.int32, (ATOMS, width), 0)
    cols = pl.ds(pl.multiple_of(first, TILE), width)
    a = pairs_ref[0:1, cols]
    b = pairs_ref[1:2, cols]
    return jnp.where(ids == a, 1.0, jnp.where(ids == b, -1.0, 0.0))


def distance(parts):
    return jnp.sqrt(parts[0] * parts[0] + parts[1] * parts[1] + parts[2] * parts[2]).astype(
        jnp.bfloat16
    )


def cov_kernel(
    weigh, *refs
):
    lag_ref, draw_ref, slot_ref, pairs_ref, *xyz_refs = refs[:-7]
    inst_ref, lagged_ref, weigh_ref, row_w_ref, col_w_ref, ds_ref, inv_ref = refs[-7:]
    frames = weigh_ref.shape[1]
    width = inst_ref.shape[2]
    lag = lag_ref[0]

    def component(k):
        return jnp.concatenate([ref[k] for ref in xyz_refs], axis=0)

    @pl.when(pl.program_id(0) == 0)
    def _():
        counts = weigh(draw_ref, slot_ref)
        t_row = lax.broadcasted_iota(jnp.int32, (BLOCK_LEN, frames), 0)
        lane = lax.broadcasted_iota(jnp.int32, (BLOCK_LEN, frames), 1)
        t_lane = lane % BLOCK_LEN
        uses_lane = jnp.where(t_lane < BLOCK_LEN - lag, 1.0, 0.0) + jnp.where(
            t_lane >= lag, 1.0, 0.0
        )
        t_col = lax.broadcasted_iota(jnp.int32, (BLOCK_LEN, 128), 0)
        uses_row = jnp.where(t_col < BLOCK_LEN - lag, 1.0, 0.0) + jnp.where(t_col >= lag, 1.0, 0.0)
        row_w = jnp.zeros((BLOCK_LEN, frames), jnp.float32)
        for b, n in enumerate(counts):
            rows = pl.ds(b * BLOCK_LEN, BLOCK_LEN)
            here = lane // BLOCK_LEN == b
            row_w = jnp.where(here, n * uses_lane, row_w)
            weigh_ref[rows, :] = jnp.where(
                here & (t_lane == t_row), n * uses_lane, 0.0
            ).astype(jnp.bfloat16)
            apart = jnp.abs(t_lane - t_row)
            weigh_ref[pl.ds(frames + b * BLOCK_LEN, BLOCK_LEN), :] = jnp.where(
                here & (apart == lag), n, 0.0
            ).astype(jnp.bfloat16)
            col_w_ref[rows, :] = (n * uses_row).astype(jnp.bfloat16)
        row_w_ref[...] = row_w[:16].astype(jnp.bfloat16)
        total = jnp.full((8, 128), (2 * DRAWS * (BLOCK_LEN - lag)).astype(jnp.float32))
        inv_ref[...] = 1.0 / total
        inv = inv_ref[0:1, 0:1]
        first = lax.axis_index("col") * width
        for j in range(width // TILE):
            signed = signed_atoms(pairs_ref, first + j * TILE, TILE).astype(jnp.bfloat16)
            f = distance([dot(component(k), signed) for k in range(3)])
            mean = dot(row_w_ref[...], f)[0:1] * inv
            c = (f.astype(jnp.float32) - mean).astype(jnp.bfloat16)
            ds_ref[:, pl.ds(j * TILE, TILE)] = (dot(weigh_ref[...], c) * inv).astype(jnp.bfloat16)

    inv = inv_ref[0:1, 0:1]
    first = lax.axis_index("row") * (pl.num_programs(0) * TILE) + pl.program_id(0) * TILE
    signed = signed_atoms(pairs_ref, first, TILE).T.astype(jnp.bfloat16)
    f = distance([dot(signed, component(k), ((1,), (1,))) for k in range(3)])
    mean = dot(f, col_w_ref[...]) * inv
    mean = jnp.concatenate([mean] * (frames // 128), axis=1)
    c = (f.astype(jnp.float32) - mean).astype(jnp.bfloat16)
    inst_ref[0] = dot(c, ds_ref[pl.ds(0, frames), :]).astype(jnp.bfloat16)
    lagged_ref[0] = dot(c, ds_ref[pl.ds(frames, frames), :]).astype(jnp.bfloat16)


def covariances(xyz, weigh, lag_time, resample, block_slot, atom_pairs):
    frames = sum(x.shape[1] for x in xyz)
    height = F // lax.axis_size("row")
    width = F // lax.axis_size("col")
    smem = pl.BlockSpec(memory_space=pltpu.SMEM)
    vmem = pl.BlockSpec(memory_space=pltpu.VMEM)
    out = jax.ShapeDtypeStruct((1, height, width), jnp.bfloat16)
    out_spec = pl.BlockSpec((1, TILE, width), lambda i: (0, i, 0))
    return pl.pallas_call(
        functools.partial(cov_kernel, weigh),
        grid=(height // TILE,),
        out_shape=(out, out),
        in_specs=[smem, smem, smem, vmem] + [vmem] * len(xyz),
        out_specs=(out_spec, out_spec),
        scratch_shapes=[
            pltpu.VMEM((2 * frames, frames), jnp.bfloat16),
            pltpu.VMEM((16, frames), jnp.bfloat16),
            pltpu.VMEM((frames, 128), jnp.bfloat16),
            pltpu.VMEM((2 * frames, width), jnp.bfloat16),
            pltpu.VMEM((8, 128), jnp.float32),
        ],
        compiler_params=pltpu.CompilerParams(vmem_limit_bytes=48 * 1024 * 1024),
        name="covariances",
    )(lag_time, resample.reshape(-1), block_slot, atom_pairs, *xyz)


def by_component(blocks):
    return blocks.transpose(2, 0, 1, 3).reshape(3, -1, ATOMS)


def shards(coordinates, resample, block_slot, lag_time, atom_pairs):
    rep_total = lax.axis_size("rep")
    blk_count = coordinates.shape[0]
    if rep_total == 2 and 2 * blk_count <= DRAWS:
        own = by_component(coordinates)
        xyz = [own, swap(own)]

        def weigh(draw_ref, slot_ref):
            mine = lax.axis_index("rep") * blk_count
            slots = [slot_ref[draw_ref[d]] for d in range(DRAWS)]
            first = [mine, blk_count - mine]
            return [
                sum(jnp.where(s == first[half] + b, 1.0, 0.0) for s in slots)
                for half in range(2)
                for b in range(blk_count)
            ]
    else:
        blocks = drawn_blocks(coordinates, resample, block_slot)
        spare = -DRAWS % (128 // BLOCK_LEN)
        blocks = jnp.pad(blocks, ((0, spare), (0, 0), (0, 0), (0, 0)))
        xyz = [by_component(blocks)]

        def weigh(draw_ref, slot_ref):
            return [1.0] * DRAWS + [0.0] * spare
    return covariances(xyz, weigh, lag_time, resample, block_slot, atom_pairs)


def solution(mesh):
    return jax.shard_map(
        shards,
        mesh=mesh,
        in_specs=(P("rep", None, None, None), P("rep", None), P(), P("rep"), P()),
        out_specs=(P("rep", "row", "col"), P("rep", "row", "col")),
        check_vma=False,
    )
```

time: 52.2 us -> 20.3 us (0.39)
  other arithmetic: 16.1 us -> 0 us
  matrix products: 13.4 us -> 0 us
  Pallas kernels: 0 us -> 13.3 us
  waiting for transfers between devices: 8.98 us -> 0 us
  blocking collectives: 5.31 us -> 0 us
  starting transfers between devices: 3.54 us -> 0 us
  local copies, waits for them, and re-layouts: 3.07 us -> 5.39 us
    dot_general x5 -> x0, matrix products: 13.4 us -> none  [the longest x1 4.66 us: shards(): jnp.einsum('na,nb->ab', row_stack, mirrored, preferred_element_type=jnp.f...]
    pallas_call x0 -> x2, Pallas kernels: none -> 13.3 us  [the longest x1 7.2 us: covariances(): pl.pallas_call(functools.partial(cov_kernel, weigh), grid=(height // TILE...]
    all_to_all x1 -> x0, waiting for transfers between devices: 8.98 us -> none  [shards(): lax.all_to_all(outgoing, 'rep', split_axis=0, concat_axis=0, tiled=True)]
    reduce_sum x5 -> x0, other arithmetic: 6.77 us -> none  [the longest x1 5.25 us: tile_features(): jnp.sum(later, axis=(0, 1))]
    all_gather x1 -> x0, blocking collectives: 5.31 us -> none  [pack_requests(): every_list = lax.all_gather(resample, 'rep', axis=0, tiled=True)]
    convert_element_type x2 -> x0, other arithmetic: 4.02 us -> none  [the longest x1 2.63 us: tile_features(): jnp.where(valid_rows, later - feature_mean, 0.0).astype(jnp.bfloat16)]
    all_to_all x1 -> x0, starting transfers between devices: 3.54 us -> none  [shards(): lax.all_to_all(outgoing, 'rep', split_axis=0, concat_axis=0, tiled=True)]
    unnamed x7 -> x10, local copies, waits for them, and re-layouts: 0.99 us -> 3.85 us
  transfers between devices with their start and end apart: 1 -> 0, of which waited for: 1 -> 0; matrix products, arithmetic and copies ran while one was open for 1% -> 0% of each run, Pallas kernels for 0% -> 0%
where the time goes in v1:
time: 20.3 us; the launch traced here: 19.9 us
  Pallas kernels  13.3 us (66%)
  local copies, waits for them, and re-layouts  5.39 us (27%)
  between operations  1.3 us (6%)
    pallas_call x1, Pallas kernels, covariances(): pl.pallas_call(functools.partial(cov_kernel, weigh), grid=(height // TILE...  7.2 us
    pallas_call x1, Pallas kernels, swap(): pl.pallas_call(swap_kernel, out_shape=jax.ShapeDtypeStruct(own.shape, own...  6.06 us
    unnamed x10, local copies, waits for them, and re-layouts  3.85 us
    transpose x1, local copies, waits for them, and re-layouts, by_component(): return blocks.transpose(2, 0, 1, 3).reshape(3, -1, ATOMS)  1.54 us

profile of v1, /device:TPU:0, one launch (start us, length us, event | category | flops | bytes accessed | tf_op | source)
XLA Modules:
  0.0 19.9 jit_solution(467392617641544027)
XLA Ops:
  1.3 1.5 %copy.7 = bf16[3,4,32,128]{3,2,1,0:T(8,128)(2,1)} copy(bf16[3,4,32,128]{3,2,0,1:T(8,128)(2,1)} %bitcast.6) | data formatting | bytes 196608 | tf_op jit(solution)/shard_map/transpose | solution.py:204
  2.8 6.1 %swap.1.refs_5_ = bf16[3,128,128]{2,1,0:T(8,128)(2,1)} custom-call(bf16[3,128,128]{2,1,0:T(8,128)(2,1)} %bitcast.3), custom_call_target="tpu_custom_call" | custom-call | tf_op jit(solution)/shard_map/swap/pallas_call | solution.py:89
  8.9 0.0 copy-start
  8.9 0.9 %copy-done = bf16[3,4,32,128]{3,2,1,0:T(8,128)(2,1)S(1)} copy-done((bf16[3,4,32,128]{3,2,1,0:T(8,128)(2,1)S(1)}, bf16[3,4,32,128]{3,2,1,0:T(8,128)(2,1)}, u32[]{:S(2)}) %copy-start) | copy-done | bytes 98328
  9.8 0.0 copy-start.1
  9.8 0.9 %copy-done.1 = bf16[3,128,128]{2,1,0:T(8,128)(2,1)S(1)} copy-done((bf16[3,128,128]{2,1,0:T(8,128)(2,1)S(1)}, bf16[3,128,128]{2,1,0:T(8,128)(2,1)}, u32[]{:S(2)}) %copy-start.1) | copy-done | bytes 98328
  10.7 0.0 copy-start.2
  10.7 0.8 %copy-done.2 = s32[2,4096]{1,0:T(2,128)S(1)} copy-done((s32[2,4096]{1,0:T(2,128)S(1)}, s32[2,4096]{1,0:T(2,128)}, u32[]{:S(2)}) %copy-start.2) | copy-done | bytes 32792
  11.4 0.0 copy-start.3
  11.4 0.7 %copy-done.3 = s32[1,22]{1,0:T(1,128)S(1)} copy-done((s32[1,22]{1,0:T(1,128)S(1)}, s32[1,22]{1,0:T(1,128)}, u32[]{:S(2)}) %copy-start.3) | copy-done | bytes 112
  12.1 0.0 copy-start.4
  12.1 0.7 %copy-done.4 = s32[8]{0:T(128)S(1)} copy-done((s32[8]{0:T(128)S(1)}, s32[8]{0:T(128)}, u32[]{:S(2)}) %copy-start.4) | copy-done | bytes 56
  12.7 7.2 %covariances.1 = (bf16[1,1024,1024]{2,1,0:T(8,128)(2,1)}, bf16[1,1024,1024]{2,1,0:T(8,128)(2,1)}) custom-call(s32[1]{0:T(128)S(6)} %copy.8.refs_0_, s32[22]{0:T(128)S(1)} %bitcast.5, s32[8]{0:T(128)S(1)} %copy-done.4, s32[2,4096]{1,0:T(2,128)S(1)} %copy-done.2, bf16[3,128,128]{2,1,0:T(8,128)(2,1)S(1)} %bitcast.4, bf16[3,128,128]{2,1,0:T(8,128)(2,1)S(1)} %copy-done.1), custom_call_target="tpu_custom_call" | custom-call | tf_op jit(solution)/shard_map/covariances/pallas_call | solution.py:185
Async XLA Ops:
  8.9 0.9 %copy-start = (bf16[3,4,32,128]{3,2,1,0:T(8,128)(2,1)S(1)}, bf16[3,4,32,128]{3,2,1,0:T(8,128)(2,1)}, u32[]{:S(2)}) copy-start(bf16[3,4,32,128]{3,2,1,0:T(8,128)(2,1)} %copy.7) | copy-start | bytes 294916
  9.8 0.9 %copy-start.1 = (bf16[3,128,128]{2,1,0:T(8,128)(2,1)S(1)}, bf16[3,128,128]{2,1,0:T(8,128)(2,1)}, u32[]{:S(2)}) copy-start(bf16[3,128,128]{2,1,0:T(8,128)(2,1)} %swap.1.refs_5_) | copy-start | bytes 294916
  10.7 0.8 %copy-start.2 = (s32[2,4096]{1,0:T(2,128)S(1)}, s32[2,4096]{1,0:T(2,128)}, u32[]{:S(2)}) copy-start(s32[2,4096]{1,0:T(2,128)} %refs_3_.1) | copy-start | bytes 98308
  11.4 0.7 %copy-start.3 = (s32[1,22]{1,0:T(1,128)S(1)}, s32[1,22]{1,0:T(1,128)}, u32[]{:S(2)}) copy-start(s32[1,22]{1,0:T(1,128)} %param.6) | copy-start | bytes 268
  12.1 0.7 %copy-start.4 = (s32[8]{0:T(128)S(1)}, s32[8]{0:T(128)}, u32[]{:S(2)}) copy-start(s32[8]{0:T(128)} %refs_2_.1) | copy-start | bytes 100

commit v2 on v0

v2 whole, which is shorter than its diff:
```python
import functools

import jax
import jax.numpy as jnp
from jax import lax
from jax.experimental import pallas as pl
from jax.experimental.pallas import tpu as pltpu
from jax.sharding import PartitionSpec as P

F = 4096
ATOMS = 128
BLOCK_LEN = 32
DRAWS = 22
TILE = 256
TINY = 1.2e-38
VMEM_BYTES = 60 * 1024 * 1024
MESH = pl.DeviceIdType.MESH


def slot_lookup(lists, slot_table):
    matches = lists[..., None] == jnp.arange(slot_table.shape[0], dtype=jnp.int32)
    return jnp.sum(jnp.where(matches, slot_table, 0), axis=-1)


def owner_rank(lists, slot_table, blk_count):
    slots = slot_lookup(lists, slot_table)
    owner_ids = slots // blk_count
    local_ids = slots % blk_count
    draw_ids = jnp.arange(lists.shape[-1], dtype=jnp.int32)
    before = (owner_ids[..., :, None] == owner_ids[..., None, :]) & (
        draw_ids[None, :] < draw_ids[:, None]
    )
    ranks = jnp.sum(before.astype(jnp.int32), axis=-1)
    return (owner_ids, local_ids, ranks)


def pack_requests(resample, block_slot, local_data, capacity):
    every_list = lax.all_gather(resample, "rep", axis=0, tiled=True)
    blk_count = local_data.shape[0]
    owners_all, local_all, ranks_all = owner_rank(every_list, block_slot, blk_count)
    myself = lax.axis_index("rep")
    wanted = (owners_all == myself)[:, :, None] & (
        ranks_all[:, :, None] == jnp.arange(capacity, dtype=jnp.int32)
    )
    picked = local_all[:, :, None] == jnp.arange(blk_count, dtype=jnp.int32)
    selector = jnp.einsum(
        "rdc,rdk->rck", wanted.astype(jnp.float32), picked.astype(jnp.float32)
    ).astype(jnp.bfloat16)
    return jnp.einsum(
        "rck,kx->rcx", selector, local_data, preferred_element_type=jnp.float32
    ).astype(jnp.bfloat16)


def unpack_blocks(received, resample, block_slot, blk_count, capacity):
    owner_ids, local_ids, ranks = owner_rank(resample[0], block_slot, blk_count)
    rows_wanted = owner_ids * capacity + ranks
    flat = received.reshape(-1, received.shape[-1])
    return jnp.take(flat, rows_wanted, axis=0)


def drawn_blocks(coordinates, resample, block_slot):
    rep_total = lax.axis_size("rep")
    per_owner = (DRAWS + rep_total - 1) // rep_total
    capacity = max(2, per_owner + per_owner // 2)
    blk_count = coordinates.shape[0]
    outgoing = pack_requests(resample, block_slot, coordinates.reshape(blk_count, -1), capacity)
    received = lax.all_to_all(outgoing, "rep", split_axis=0, concat_axis=0, tiled=True)
    return unpack_blocks(received, resample, block_slot, blk_count, capacity).reshape(
        DRAWS, BLOCK_LEN, 3, ATOMS
    )


def dot(a, b):
    return jnp.dot(a, b, preferred_element_type=jnp.float32)


def signed_atoms(pairs_ref, first):
    ids = lax.broadcasted_iota(jnp.int32, (ATOMS, TILE), 0)
    cols = pl.ds(pl.multiple_of(first, TILE), TILE)
    a = pairs_ref[0:1, cols]
    b = pairs_ref[1:2, cols]
    return jnp.where(ids == a, 1.0, jnp.where(ids == b, -1.0, 0.0)).astype(jnp.bfloat16)


def features(blocks_ref, signed):
    squared = 0.0
    for k in range(3):
        difference = dot(blocks_ref[:, k].reshape(-1, ATOMS), signed)
        squared = squared + difference * difference
    return (squared * lax.rsqrt(jnp.maximum(squared, TINY))).astype(jnp.bfloat16)


def near_kernel(partnered, weigh, *refs):
    outs, scratch = refs[5:-11], refs[-11:]
    lag_ref = refs[4]
    blocks_ref, draw_ref, slot_ref, pairs_ref = scratch[:4]
    built = col_ref, row_ref, weigh_ref, inv_ref = scratch[4:8]
    sems, send_sem, recv_sem = scratch[8:]
    frames = weigh_ref.shape[1]

    if partnered:
        partner = {"rep": 1 - lax.axis_index("rep")}
        barrier = pltpu.get_barrier_semaphore()
        pl.semaphore_signal(barrier, inc=1, device_id=partner, device_id_type=MESH)
    fetches = [
        pltpu.make_async_copy(src, dst, sems.at[i])
        for i, (src, dst) in enumerate(zip(refs[:4], scratch[:4]))
    ]
    for fetch in fetches:
        fetch.start()
    if partnered:
        pl.semaphore_wait(barrier, 1)
        copy = pltpu.make_async_remote_copy(
            src_ref=refs[0],
            dst_ref=outs[4],
            send_sem=send_sem,
            recv_sem=recv_sem,
            device_id=partner,
            device_id_type=MESH,
        )
        copy.start()
    for fetch in fetches:
        fetch.wait()

    stores = [
        pltpu.make_async_copy(src, dst, sems.at[4 + i])
        for i, (src, dst) in enumerate(zip(built, outs[:4]))
    ]
    for i, axis in enumerate(("col", "row")):
        side_ref = built[i]
        width = side_ref.shape[1]
        for j in range(width // TILE):
            cols = pl.ds(j * TILE, TILE)
            signed = signed_atoms(pairs_ref, lax.axis_index(axis) * width + j * TILE)
            side_ref[:ATOMS, cols] = signed
            side_ref[ATOMS:, cols] = features(blocks_ref, signed)
        stores[i].start()

    lag = lag_ref[0]
    counts = weigh(draw_ref, slot_ref)
    t_row = lax.broadcasted_iota(jnp.int32, (BLOCK_LEN, frames), 0)
    lane = lax.broadcasted_iota(jnp.int32, (BLOCK_LEN, frames), 1)
    t_lane = lane % BLOCK_LEN
    uses = jnp.where(t_lane < BLOCK_LEN - lag, 1.0, 0.0) + jnp.where(t_lane >= lag, 1.0, 0.0)
    same = jnp.where(t_lane == t_row, uses, 0.0)
    apart = jnp.where(jnp.abs(t_lane - t_row) == lag, 1.0, 0.0)
    mean_w = jnp.zeros((BLOCK_LEN, frames), jnp.float32)
    for b, n in enumerate(counts):
        share = jnp.where(lane // BLOCK_LEN == b, n, 0.0)
        mean_w = mean_w + share * uses
        weigh_ref[pl.ds(b * BLOCK_LEN, BLOCK_LEN), :] = (share * same).astype(jnp.bfloat16)
        weigh_ref[pl.ds(frames + b * BLOCK_LEN, BLOCK_LEN), :] = (share * apart).astype(
            jnp.bfloat16
        )
    weigh_ref[pl.ds(2 * frames, 16), :] = mean_w[:16].astype(jnp.bfloat16)
    inv_ref[...] = 1.0 / jnp.full((8, 128), (2 * DRAWS * (BLOCK_LEN - lag)).astype(jnp.float32))
    for store in stores[2:]:
        store.start()
    for store in stores:
        store.wait()
    if partnered:
        copy.wait()


def near_side(blocks, partnered, weigh, lag_time, resample, block_slot, atom_pairs):
    held = blocks.shape[0] * BLOCK_LEN
    frames = held * (2 if partnered else 1)
    built = [
        ((ATOMS + held, F // lax.axis_size("col")), jnp.bfloat16),
        ((ATOMS + held, F // lax.axis_size("row")), jnp.bfloat16),
        ((2 * frames + 16, frames), jnp.bfloat16),
        ((8, 128), jnp.float32),
    ]
    outs = [jax.ShapeDtypeStruct(*shape) for shape in built]
    if partnered:
        outs.append(jax.ShapeDtypeStruct(blocks.shape, blocks.dtype))
    return pl.pallas_call(
        functools.partial(near_kernel, partnered, weigh),
        out_shape=outs,
        in_specs=[pl.BlockSpec(memory_space=pltpu.HBM)] * 4
        + [pl.BlockSpec(memory_space=pltpu.SMEM)],
        out_specs=[pl.BlockSpec(memory_space=pltpu.HBM)] * len(outs),
        scratch_shapes=[
            pltpu.VMEM(blocks.shape, blocks.dtype),
            pltpu.SMEM(resample.shape, jnp.int32),
            pltpu.SMEM(block_slot.shape, jnp.int32),
            pltpu.VMEM(atom_pairs.shape, jnp.int32),
            *[pltpu.VMEM(*shape) for shape in built],
            pltpu.SemaphoreType.DMA((8,)),
            pltpu.SemaphoreType.DMA,
            pltpu.SemaphoreType.DMA,
        ],
        compiler_params=pltpu.CompilerParams(
            vmem_limit_bytes=VMEM_BYTES,
            **(dict(collective_id=0, has_side_effects=True) if partnered else {}),
        ),
        name="near_side",
    )(blocks, resample, block_slot, atom_pairs, lag_time)


def cov_kernel(inputs, *refs):
    inst_ref, lagged_ref = refs[inputs : inputs + 2]
    held_refs, ds_ref, sems = refs[inputs + 2 : -2], refs[-2], refs[-1]
    col_ref, row_ref, weigh_ref, inv_ref, *far_refs = held_refs
    frames = weigh_ref.shape[1]

    def centred(side_ref, first):
        cols = pl.ds(pl.multiple_of(first, TILE), TILE)
        parts = [side_ref[ATOMS:, cols]]
        parts += [features(far_ref, side_ref[:ATOMS, cols]) for far_ref in far_refs]
        f = jnp.concatenate(parts, axis=0)
        mean = dot(weigh_ref[pl.ds(2 * frames, 16), :], f)[0:1] * inv_ref[0:1, 0:1]
        return f.astype(jnp.float32) - mean

    @pl.when(pl.program_id(0) == 0)
    def _():
        fetches = [
            pltpu.make_async_copy(refs[i], held_refs[i], sems.at[i]) for i in range(inputs)
        ]
        order = [i for i in range(inputs) if i != 1]
        for i in order + [1]:
            fetches[i].start()
        for i in order:
            fetches[i].wait()
        for j in range(ds_ref.shape[1] // TILE):
            c = centred(col_ref, j * TILE).astype(jnp.bfloat16)
            ds_ref[:, pl.ds(j * TILE, TILE)] = (
                dot(weigh_ref[pl.ds(0, 2 * frames), :], c) * inv_ref[0:1, 0:1]
            ).astype(jnp.bfloat16)
        fetches[1].wait()

    c = centred(row_ref, pl.program_id(0) * TILE).T.astype(jnp.bfloat16)
    inst_ref[0] = dot(c, ds_ref[pl.ds(0, frames), :]).astype(jnp.bfloat16)
    lagged_ref[0] = dot(c, ds_ref[pl.ds(frames, frames), :]).astype(jnp.bfloat16)


def covariances(sides):
    frames = sides[2].shape[1]
    height = F // lax.axis_size("row")
    width = F // lax.axis_size("col")
    out = jax.ShapeDtypeStruct((1, height, width), jnp.bfloat16)
    out_spec = pl.BlockSpec((1, TILE, width), lambda i: (0, i, 0))
    return pl.pallas_call(
        functools.partial(cov_kernel, len(sides)),
        grid=(height // TILE,),
        out_shape=(out, out),
        in_specs=[pl.BlockSpec(memory_space=pltpu.HBM)] * len(sides),
        out_specs=(out_spec, out_spec),
        scratch_shapes=[
            *[pltpu.VMEM(side.shape, side.dtype) for side in sides],
            pltpu.VMEM((2 * frames, width), jnp.bfloat16),
            pltpu.SemaphoreType.DMA((len(sides),)),
        ],
        compiler_params=pltpu.CompilerParams(vmem_limit_bytes=VMEM_BYTES),
        name="covariances",
    )(*sides)


def shards(coordinates, resample, block_slot, lag_time, atom_pairs):
    blk_count = coordinates.shape[0]
    partnered = lax.axis_size("rep") == 2 and 2 * blk_count <= DRAWS
    if partnered:
        blocks = coordinates

        def weigh(draw_ref, slot_ref):
            mine = lax.axis_index("rep") * blk_count
            slots = [slot_ref[draw_ref[0, d]] for d in range(DRAWS)]
            return [
                sum(jnp.where(s == first + b, 1.0, 0.0) for s in slots)
                for first in (mine, blk_count - mine)
                for b in range(blk_count)
            ]
    else:
        spare = -DRAWS % (128 // BLOCK_LEN)
        blocks = drawn_blocks(coordinates, resample, block_slot)
        blocks = jnp.pad(blocks, ((0, spare), (0, 0), (0, 0), (0, 0)))

        def weigh(draw_ref, slot_ref):
            return [1.0] * DRAWS + [0.0] * spare
    sides = near_side(
        blocks.transpose(0, 2, 1, 3), partnered, weigh, lag_time, resample, block_slot, atom_pairs
    )
    return covariances(sides)


def solution(mesh):
    return jax.shard_map(
        shards,
        mesh=mesh,
        in_specs=(P("rep", None, None, None), P("rep", None), P(), P("rep"), P()),
        out_specs=(P("rep", "row", "col"), P("rep", "row", "col")),
        check_vma=False,
    )
```

time: 52.2 us -> 14.4 us (0.28)
  other arithmetic: 16.1 us -> 0 us
  matrix products: 13.4 us -> 0 us
  Pallas kernels: 0 us -> 13 us
  waiting for transfers between devices: 8.98 us -> 0 us
  blocking collectives: 5.31 us -> 0 us
  starting transfers between devices: 3.54 us -> 0 us
  local copies, waits for them, and re-layouts: 3.07 us -> 0 us
    dot_general x5 -> x0, matrix products: 13.4 us -> none  [the longest x1 4.66 us: shards(): jnp.einsum('na,nb->ab', row_stack, mirrored, preferred_element_type=jnp.f...]
    pallas_call x0 -> x2, Pallas kernels: none -> 13 us  [the longest x1 6.73 us: covariances(): pl.pallas_call(functools.partial(cov_kernel, len(sides)), grid=(height //...]
    all_to_all x1 -> x0, waiting for transfers between devices: 8.98 us -> none  [shards(): lax.all_to_all(outgoing, 'rep', split_axis=0, concat_axis=0, tiled=True)]
    reduce_sum x5 -> x0, other arithmetic: 6.77 us -> none  [the longest x1 5.25 us: tile_features(): jnp.sum(later, axis=(0, 1))]
    all_gather x1 -> x0, blocking collectives: 5.31 us -> none  [pack_requests(): every_list = lax.all_gather(resample, 'rep', axis=0, tiled=True)]
    convert_element_type x2 -> x0, other arithmetic: 4.02 us -> none  [the longest x1 2.63 us: tile_features(): jnp.where(valid_rows, later - feature_mean, 0.0).astype(jnp.bfloat16)]
    all_to_all x1 -> x0, starting transfers between devices: 3.54 us -> none  [shards(): lax.all_to_all(outgoing, 'rep', split_axis=0, concat_axis=0, tiled=True)]
    another operation x2 -> x0, other arithmetic: 2.4 us -> none
  transfers between devices with their start and end apart: 1 -> 0, of which waited for: 1 -> 0; matrix products, arithmetic and copies ran while one was open for 1% -> 0% of each run, Pallas kernels for 0% -> 0%
where the time goes in v2:
time: 14.4 us; the launch traced here: 14.3 us
  Pallas kernels  13 us (90%)
  between operations  1.28 us (9%)
    pallas_call x1, Pallas kernels, covariances(): pl.pallas_call(functools.partial(cov_kernel, len(sides)), grid=(height //...  6.73 us
    pallas_call x1, Pallas kernels, near_side(): pl.pallas_call(functools.partial(near_kernel, partnered, weigh), out_shap...  6.25 us

profile of v2, /device:TPU:0, one launch (start us, length us, event | category | flops | bytes accessed | tf_op | source)
XLA Modules:
  0.0 14.3 jit_solution(4420611269551959076)
XLA Ops:
  1.3 6.2 %near_side.1 = (bf16[256,1024]{1,0:T(8,128)(2,1)}, bf16[256,1024]{1,0:T(8,128)(2,1)}, bf16[528,256]{1,0:T(8,128)(2,1)}, f32[8,128]{1,0:T(8,128)}, bf16[4,3,32,128]{3,2,1,0:T(8,128)(2,1)}) custom-call(bf16[4,3,32,128]{3,2,1,0:T(8,128)(2,1)} %bitcast.1, s32[1,22]{1,0:T(1,128)} %refs_1_.1, s32[8]{0:T(128)} %refs_2_.1, s32[2,4096]{1,0:T(2,128)} %refs_3_.1, ...), custom_call_target="tpu_custom_call" | custom-call | tf_op jit(solution)/shard_map/near_side/pallas_call | solution.py:177
  7.5 6.7 %covariances.1 = (bf16[1,1024,1024]{2,1,0:T(8,128)(2,1)}, bf16[1,1024,1024]{2,1,0:T(8,128)(2,1)}) custom-call(bf16[256,1024]{1,0:T(8,128)(2,1)} %get-tuple-element.7.refs_0_, bf16[256,1024]{1,0:T(8,128)(2,1)} %get-tuple-element.8.refs_1_, bf16[528,256]{1,0:T(8,128)(2,1)} %get-tuple-element.9.refs_2_, f32[8,128]{1,0:T(8,128)} %get-tuple-element.10.refs_3_, ...), custom_call_target="tpu_custom_call" | custom-call | tf_op jit(solution)/shard_map/covariances/pallas_call | solution.py:243

commit v3 on v2

--- a/solution.py
+++ b/solution.py
@@ -200,38 +200,52 @@
 
 def cov_kernel(inputs, *refs):
     inst_ref, lagged_ref = refs[inputs : inputs + 2]
-    held_refs, ds_ref, sems = refs[inputs + 2 : -2], refs[-2], refs[-1]
+    held_refs = refs[inputs + 2 : -4]
+    c_ref, turned_ref, ds_ref, sems = refs[-4:]
     col_ref, row_ref, weigh_ref, inv_ref, *far_refs = held_refs
     frames = weigh_ref.shape[1]
-
-    def centred(side_ref, first):
-        cols = pl.ds(pl.multiple_of(first, TILE), TILE)
-        parts = [side_ref[ATOMS:, cols]]
-        parts += [features(far_ref, side_ref[:ATOMS, cols]) for far_ref in far_refs]
-        f = jnp.concatenate(parts, axis=0)
-        mean = dot(weigh_ref[pl.ds(2 * frames, 16), :], f)[0:1] * inv_ref[0:1, 0:1]
-        return f.astype(jnp.float32) - mean
+    inv = lambda: inv_ref[0:1, 0:1]
 
     @pl.when(pl.program_id(0) == 0)
     def _():
         fetches = [
-            pltpu.make_async_copy(refs[i], held_refs[i], sems.at[i]) for i in range(inputs)
+            pltpu.make_async_copy(
+                src, dst.at[pl.ds(0, src.shape[0])] if i < 2 else dst, sems.at[i]
+            )
+            for i, (src, dst) in enumerate(zip(refs[:inputs], held_refs))
         ]
-        order = [i for i in range(inputs) if i != 1]
-        for i in order + [1]:
-            fetches[i].start()
-        for i in order:
-            fetches[i].wait()
-        for j in range(ds_ref.shape[1] // TILE):
-            c = centred(col_ref, j * TILE).astype(jnp.bfloat16)
-            ds_ref[:, pl.ds(j * TILE, TILE)] = (
-                dot(weigh_ref[pl.ds(0, 2 * frames), :], c) * inv_ref[0:1, 0:1]
+        for fetch in fetches:
+            fetch.start()
+        for fetch in fetches:
+            fetch.wait()
+        for side_ref in (col_ref, row_ref):
+            for j in range(side_ref.shape[1] // TILE):
+                cols = pl.ds(j * TILE, TILE)
+                at = ATOMS + frames - len(far_refs) * (frames // 2)
+                for far_ref in far_refs:
+                    side_ref[at:, cols] = features(far_ref, side_ref[:ATOMS, cols])
+        mean_w = weigh_ref[pl.ds(2 * frames, 16), :]
+        means = [
+            dot(mean_w, side_ref[ATOMS:, :])[0:1] * inv() for side_ref in (col_ref, row_ref)
+        ]
+        for j in range(ds_ref.shape[0]):
+            cols = pl.ds(j * TILE, TILE)
+            f = col_ref[ATOMS:, cols].astype(jnp.float32)
+            c_ref[:, cols] = (f - means[0][:, j * TILE : (j + 1) * TILE]).astype(jnp.bfloat16)
+        for j in range(turned_ref.shape[0] // TILE):
+            cols = pl.ds(j * TILE, TILE)
+            f = row_ref[ATOMS:, cols].astype(jnp.float32)
+            c = (f - means[1][:, j * TILE : (j + 1) * TILE]).astype(jnp.bfloat16)
+            turned_ref[cols, :] = c.T
+        for j in range(ds_ref.shape[0]):
+            ds_ref[j] = (
+                dot(weigh_ref[pl.ds(0, 2 * frames), :], c_ref[:, pl.ds(j * TILE, TILE)]) * inv()
             ).astype(jnp.bfloat16)
-        fetches[1].wait()
-
-    c = centred(row_ref, pl.program_id(0) * TILE).T.astype(jnp.bfloat16)
-    inst_ref[0] = dot(c, ds_ref[pl.ds(0, frames), :]).astype(jnp.bfloat16)
-    lagged_ref[0] = dot(c, ds_ref[pl.ds(frames, frames), :]).astype(jnp.bfloat16)
+
+    j = pl.program_id(0)
+    c = turned_ref[...]
+    inst_ref[0] = dot(c, ds_ref[j, pl.ds(0, frames), :]).astype(jnp.bfloat16)
+    lagged_ref[0] = dot(c, ds_ref[j, pl.ds(frames, frames), :]).astype(jnp.bfloat16)
 
 
 def covariances(sides):
@@ -239,16 +253,20 @@
     height = F // lax.axis_size("row")
     width = F // lax.axis_size("col")
     out = jax.ShapeDtypeStruct((1, height, width), jnp.bfloat16)
-    out_spec = pl.BlockSpec((1, TILE, width), lambda i: (0, i, 0))
+    out_spec = pl.BlockSpec((1, height, TILE), lambda j: (0, 0, j))
     return pl.pallas_call(
         functools.partial(cov_kernel, len(sides)),
-        grid=(height // TILE,),
+        grid=(width // TILE,),
         out_shape=(out, out),
         in_specs=[pl.BlockSpec(memory_space=pltpu.HBM)] * len(sides),
         out_specs=(out_spec, out_spec),
         scratch_shapes=[
-            *[pltpu.VMEM(side.shape, side.dtype) for side in sides],
-            pltpu.VMEM((2 * frames, width), jnp.bfloat16),
+            pltpu.VMEM((ATOMS + frames, width), jnp.bfloat16),
+            pltpu.VMEM((ATOMS + frames, height), jnp.bfloat16),
+            *[pltpu.VMEM(side.shape, side.dtype) for side in sides[2:]],
+            pltpu.VMEM((frames, width), jnp.bfloat16),
+            pltpu.VMEM((height, frames), jnp.bfloat16),
+            pltpu.VMEM((width // TILE, 2 * frames, TILE), jnp.bfloat16),
             pltpu.SemaphoreType.DMA((len(sides),)),
         ],
         compiler_params=pltpu.CompilerParams(vmem_limit_bytes=VMEM_BYTES),

time: 14.4 us -> 13.3 us (0.924)
  Pallas kernels: 13 us -> 11.9 us
    pallas_call x1, Pallas kernels: 6.73 us -> 5.64 us  [covariances(): pl.pallas_call(functools.partial(cov_kernel, len(sides)), grid=(width //...]
where the time goes in v3:
time: 13.3 us; the launch traced here: 13.2 us
  Pallas kernels  11.9 us (89%)
  between operations  1.28 us (10%)
    pallas_call x1, Pallas kernels, near_side(): pl.pallas_call(functools.partial(near_kernel, partnered, weigh), out_shap...  6.25 us
    pallas_call x1, Pallas kernels, covariances(): pl.pallas_call(functools.partial(cov_kernel, len(sides)), grid=(width //...  5.64 us

profile of v3, /device:TPU:0, one launch (start us, length us, event | category | flops | bytes accessed | tf_op | source)
XLA Modules:
  0.0 13.2 jit_solution(9855055683436189771)
XLA Ops:
  1.3 6.2 %near_side.1 = (bf16[256,1024]{1,0:T(8,128)(2,1)}, bf16[256,1024]{1,0:T(8,128)(2,1)}, bf16[528,256]{1,0:T(8,128)(2,1)}, f32[8,128]{1,0:T(8,128)}, bf16[4,3,32,128]{3,2,1,0:T(8,128)(2,1)}) custom-call(bf16[4,3,32,128]{3,2,1,0:T(8,128)(2,1)} %bitcast.1, s32[1,22]{1,0:T(1,128)} %refs_1_.1, s32[8]{0:T(128)} %refs_2_.1, s32[2,4096]{1,0:T(2,128)} %refs_3_.1, ...), custom_call_target="tpu_custom_call" | custom-call | tf_op jit(solution)/shard_map/near_side/pallas_call | solution.py:177
  7.5 5.6 %covariances.1 = (bf16[1,1024,1024]{2,1,0:T(8,128)(2,1)}, bf16[1,1024,1024]{2,1,0:T(8,128)(2,1)}) custom-call(bf16[256,1024]{1,0:T(8,128)(2,1)} %get-tuple-element.7.refs_0_, bf16[256,1024]{1,0:T(8,128)(2,1)} %get-tuple-element.8.refs_1_, bf16[528,256]{1,0:T(8,128)(2,1)} %get-tuple-element.9.refs_2_, f32[8,128]{1,0:T(8,128)} %get-tuple-element.10.refs_3_, ...), custom_call_target="tpu_custom_call" | custom-call | tf_op jit(solution)/shard_map/covariances/pallas_call | solution.py:257

commit v4 on v3

--- a/solution.py
+++ b/solution.py
@@ -101,7 +101,11 @@
     if partnered:
         partner = {"rep": 1 - lax.axis_index("rep")}
         barrier = pltpu.get_barrier_semaphore()
-        pl.semaphore_signal(barrier, inc=1, device_id=partner, device_id_type=MESH)
+        me = lax.axis_index("col")
+        part = me % 2
+        twin = {"col": me + 1 - 2 * part}
+        for other in (partner, twin):
+            pl.semaphore_signal(barrier, inc=1, device_id=other, device_id_type=MESH)
     fetches = [
         pltpu.make_async_copy(src, dst, sems.at[i])
         for i, (src, dst) in enumerate(zip(refs[:4], scratch[:4]))
@@ -109,15 +113,20 @@
     for fetch in fetches:
         fetch.start()
     if partnered:
-        pl.semaphore_wait(barrier, 1)
-        copy = pltpu.make_async_remote_copy(
-            src_ref=refs[0],
-            dst_ref=outs[4],
-            send_sem=send_sem,
-            recv_sem=recv_sem,
-            device_id=partner,
-            device_id_type=MESH,
-        )
+        pl.semaphore_wait(barrier, 2)
+        half = refs[0].shape[0] // 2
+        mine = pl.ds(part * half, half)
+        copy, forward = [
+            pltpu.make_async_remote_copy(
+                src_ref=src.at[mine],
+                dst_ref=outs[4].at[mine],
+                send_sem=send_sem.at[i],
+                recv_sem=recv_sem.at[i],
+                device_id=other,
+                device_id_type=MESH,
+            )
+            for i, (src, other) in enumerate(((refs[0], partner), (outs[4], twin)))
+        ]
         copy.start()
     for fetch in fetches:
         fetch.wait()
@@ -135,6 +144,9 @@
             side_ref[:ATOMS, cols] = signed
             side_ref[ATOMS:, cols] = features(blocks_ref, signed)
         stores[i].start()
+        if partnered and i == 0:
+            copy.wait_recv()
+            forward.start()
 
     lag = lag_ref[0]
     counts = weigh(draw_ref, slot_ref)
@@ -159,7 +171,8 @@
     for store in stores:
         store.wait()
     if partnered:
-        copy.wait()
+        copy.wait_send()
+        forward.wait()
 
 
 def near_side(blocks, partnered, weigh, lag_time, resample, block_slot, atom_pairs):
@@ -187,8 +200,8 @@
             pltpu.VMEM(atom_pairs.shape, jnp.int32),
             *[pltpu.VMEM(*shape) for shape in built],
             pltpu.SemaphoreType.DMA((8,)),
-            pltpu.SemaphoreType.DMA,
-            pltpu.SemaphoreType.DMA,
+            pltpu.SemaphoreType.DMA((2,)),
+            pltpu.SemaphoreType.DMA((2,)),
         ],
         compiler_params=pltpu.CompilerParams(
             vmem_limit_bytes=VMEM_BYTES,
@@ -214,16 +227,19 @@
             )
             for i, (src, dst) in enumerate(zip(refs[:inputs], held_refs))
         ]
-        for fetch in fetches:
+        for fetch in fetches[4:] + fetches[:4]:
             fetch.start()
-        for fetch in fetches:
+        for fetch in fetches[4:]:
             fetch.wait()
-        for side_ref in (col_ref, row_ref):
+        for fetch, side_ref in zip(fetches, (col_ref, row_ref)):
+            fetch.wait()
             for j in range(side_ref.shape[1] // TILE):
                 cols = pl.ds(j * TILE, TILE)
                 at = ATOMS + frames - len(far_refs) * (frames // 2)
                 for far_ref in far_refs:
                     side_ref[at:, cols] = features(far_ref, side_ref[:ATOMS, cols])
+        for fetch in fetches[2:4]:
+            fetch.wait()
         mean_w = weigh_ref[pl.ds(2 * frames, 16), :]
         means = [
             dot(mean_w, side_ref[ATOMS:, :])[0:1] * inv() for side_ref in (col_ref, row_ref)
@@ -276,7 +292,8 @@
 
 def shards(coordinates, resample, block_slot, lag_time, atom_pairs):
     blk_count = coordinates.shape[0]
-    partnered = lax.axis_size("rep") == 2 and 2 * blk_count <= DRAWS
+    halves = blk_count % 2 == 0 and lax.axis_size("col") % 2 == 0
+    partnered = lax.axis_size("rep") == 2 and 2 * blk_count <= DRAWS and halves
     if partnered:
         blocks = coordinates
 

time: 13.3 us -> 14.4 us (1.083)
  Pallas kernels: 11.9 us -> 12.9 us
    pallas_call x1, Pallas kernels: 6.25 us -> 7.16 us  [near_side(): pl.pallas_call(functools.partial(near_kernel, partnered, weigh), out_shap...]
where the time goes in v4:
time: 14.4 us; the launch traced here: 14.2 us
  Pallas kernels  12.9 us (90%)
  between operations  1.28 us (9%)
    pallas_call x1, Pallas kernels, near_side(): pl.pallas_call(functools.partial(near_kernel, partnered, weigh), out_shap...  7.16 us
    pallas_call x1, Pallas kernels, covariances(): pl.pallas_call(functools.partial(cov_kernel, len(sides)), grid=(width //...  5.76 us

profile of v4, /device:TPU:0, one launch (start us, length us, event | category | flops | bytes accessed | tf_op | source)
XLA Modules:
  0.0 14.2 jit_solution(11675860469648973025)
XLA Ops:
  1.3 7.2 %near_side.1 = (bf16[256,1024]{1,0:T(8,128)(2,1)}, bf16[256,1024]{1,0:T(8,128)(2,1)}, bf16[528,256]{1,0:T(8,128)(2,1)}, f32[8,128]{1,0:T(8,128)}, bf16[4,3,32,128]{3,2,1,0:T(8,128)(2,1)}) custom-call(bf16[4,3,32,128]{3,2,1,0:T(8,128)(2,1)} %bitcast.1, s32[1,22]{1,0:T(1,128)} %refs_1_.1, s32[8]{0:T(128)} %refs_2_.1, s32[2,4096]{1,0:T(2,128)} %refs_3_.1, ...), custom_call_target="tpu_custom_call" | custom-call | tf_op jit(solution)/shard_map/near_side/pallas_call | solution.py:190
  8.4 5.8 %covariances.1 = (bf16[1,1024,1024]{2,1,0:T(8,128)(2,1)}, bf16[1,1024,1024]{2,1,0:T(8,128)(2,1)}) custom-call(bf16[256,1024]{1,0:T(8,128)(2,1)} %get-tuple-element.7.refs_0_, bf16[256,1024]{1,0:T(8,128)(2,1)} %get-tuple-element.8.refs_1_, bf16[528,256]{1,0:T(8,128)(2,1)} %get-tuple-element.9.refs_2_, f32[8,128]{1,0:T(8,128)} %get-tuple-element.10.refs_3_, ...), custom_call_target="tpu_custom_call" | custom-call | tf_op jit(solution)/shard_map/covariances/pallas_call | solution.py:273

commit v5 on v3

--- a/solution.py
+++ b/solution.py
@@ -242,10 +242,13 @@
                 dot(weigh_ref[pl.ds(0, 2 * frames), :], c_ref[:, pl.ds(j * TILE, TILE)]) * inv()
             ).astype(jnp.bfloat16)
 
-    j = pl.program_id(0)
+    tiles = inst_ref.shape[2] // TILE
     c = turned_ref[...]
-    inst_ref[0] = dot(c, ds_ref[j, pl.ds(0, frames), :]).astype(jnp.bfloat16)
-    lagged_ref[0] = dot(c, ds_ref[j, pl.ds(frames, frames), :]).astype(jnp.bfloat16)
+    for i in range(tiles):
+        j = pl.program_id(0) * tiles + i
+        cols = pl.ds(i * TILE, TILE)
+        inst_ref[0, :, cols] = dot(c, ds_ref[j, pl.ds(0, frames), :]).astype(jnp.bfloat16)
+        lagged_ref[0, :, cols] = dot(c, ds_ref[j, pl.ds(frames, frames), :]).astype(jnp.bfloat16)
 
 
 def covariances(sides):
@@ -253,10 +256,10 @@
     height = F // lax.axis_size("row")
     width = F // lax.axis_size("col")
     out = jax.ShapeDtypeStruct((1, height, width), jnp.bfloat16)
-    out_spec = pl.BlockSpec((1, height, TILE), lambda j: (0, 0, j))
+    out_spec = pl.BlockSpec((1, height, 2 * TILE), lambda j: (0, 0, j))
     return pl.pallas_call(
         functools.partial(cov_kernel, len(sides)),
-        grid=(width // TILE,),
+        grid=(width // (2 * TILE),),
         out_shape=(out, out),
         in_specs=[pl.BlockSpec(memory_space=pltpu.HBM)] * len(sides),
         out_specs=(out_spec, out_spec),

time: 13.3 us -> 12.8 us (0.962)
  Pallas kernels: 11.9 us -> 11.4 us
    pallas_call x1, Pallas kernels: 5.64 us -> 5.14 us  [covariances(): pl.pallas_call(functools.partial(cov_kernel, len(sides)), grid=(width //...]
where the time goes in v5:
time: 12.8 us; the launch traced here: 12.7 us
  Pallas kernels  11.4 us (89%)
  between operations  1.28 us (10%)
    pallas_call x1, Pallas kernels, near_side(): pl.pallas_call(functools.partial(near_kernel, partnered, weigh), out_shap...  6.25 us
    pallas_call x1, Pallas kernels, covariances(): pl.pallas_call(functools.partial(cov_kernel, len(sides)), grid=(width //...  5.14 us

profile of v5, /device:TPU:0, one launch (start us, length us, event | category | flops | bytes accessed | tf_op | source)
XLA Modules:
  0.0 12.7 jit_solution(15756711329491865729)
XLA Ops:
  1.3 6.2 %near_side.1 = (bf16[256,1024]{1,0:T(8,128)(2,1)}, bf16[256,1024]{1,0:T(8,128)(2,1)}, bf16[528,256]{1,0:T(8,128)(2,1)}, f32[8,128]{1,0:T(8,128)}, bf16[4,3,32,128]{3,2,1,0:T(8,128)(2,1)}) custom-call(bf16[4,3,32,128]{3,2,1,0:T(8,128)(2,1)} %bitcast.1, s32[1,22]{1,0:T(1,128)} %refs_1_.1, s32[8]{0:T(128)} %refs_2_.1, s32[2,4096]{1,0:T(2,128)} %refs_3_.1, ...), custom_call_target="tpu_custom_call" | custom-call | tf_op jit(solution)/shard_map/near_side/pallas_call | solution.py:177
  7.5 5.1 %covariances.1 = (bf16[1,1024,1024]{2,1,0:T(8,128)(2,1)}, bf16[1,1024,1024]{2,1,0:T(8,128)(2,1)}) custom-call(bf16[256,1024]{1,0:T(8,128)(2,1)} %get-tuple-element.7.refs_0_, bf16[256,1024]{1,0:T(8,128)(2,1)} %get-tuple-element.8.refs_1_, bf16[528,256]{1,0:T(8,128)(2,1)} %get-tuple-element.9.refs_2_, f32[8,128]{1,0:T(8,128)} %get-tuple-element.10.refs_3_, ...), custom_call_target="tpu_custom_call" | custom-call | tf_op jit(solution)/shard_map/covariances/pallas_call | solution.py:260
